TPU v7x, 256 devices: a whole 4x4x8 slice. The times are simulated.
256 devices in a mesh: ctx: 64 (over x, z, y_hi), tp: 4 (over y_lo, core).
Axes of the slice: x: 4, y: 4 (y_hi: 2, y_lo: 2; y = y_hi * 2 + y_lo), z: 8, core: 2. Of those that a mesh axis runs over, the one named last changes fastest.
Arguments:
- queries: bfloat16 [65536, 2048], P('ctx', 'tp'), may hold values from -6 to 6
- keys: bfloat16 [65536, 2048], P('ctx', 'tp'), may hold values from -6 to 6
- values: bfloat16 [65536, 2048], P('ctx', 'tp'), may hold values from -6 to 6
- offsets: int32 [32, 2], replicated, may hold values from 0 to 15
- out_weight: bfloat16 [2048, 2048], P('tp'), may hold values from -0.125 to 0.125
Outputs:
- mixed: bfloat16 [65536, 2048], P(('ctx', 'tp'))
All inputs are finite; a program needn't handle non-finite values.
Results may differ from a plain program's by a relative error of at most 0.015.
Values may be sent and summed in bfloat16 or wider, within the bound.
No kernel may reach another device: no remote copies, remote signals or barrier semaphores. Data moves between devices by JAX's collectives and lax.ppermute only.
A program may use at most 128 MiB of HBM per device.

v0:
```python
import jax
import jax.numpy as jnp
from jax import lax
from jax.sharding import PartitionSpec as P

HEAD_DIM = 64
SECOND_DILATION = 8
SPAN_BITS = 3
THIRD_DILATION = 16
NEG = -1e30


def partner_2(shard, axis, stride):
    return lax.ppermute(shard, axis, [(i, i ^ 1 << stride) for i in range(lax.axis_size(axis))])


def select_rows(field, dilation, start_offset, heads_on_shard):
    count_of_rows = field.shape[0]
    shaped = field.reshape(count_of_rows // dilation, dilation, heads_on_shard, HEAD_DIM)
    picked = lax.broadcasted_iota(
        jnp.int32, (1, dilation, heads_on_shard, 1), 1
    ) == start_offset.reshape(1, 1, heads_on_shard, 1)
    return jnp.sum(jnp.where(picked, shaped, jnp.zeros_like(shaped)), axis=1)


def attend(inputs):
    query_per_head, key_per_head, value_per_head = inputs
    scores = jnp.dot(
        query_per_head, key_per_head.T, preferred_element_type=jnp.float32
    ) * HEAD_DIM ** (-0.5)
    peak = jnp.max(scores, axis=1)
    expo = jnp.exp(scores - peak[:, None])
    total = jnp.sum(expo, axis=1)
    summed = jnp.dot(expo.astype(jnp.bfloat16), value_per_head, preferred_element_type=jnp.float32)
    return (peak, total, summed)


def widen_pattern(peak, total, summed, dilation, start_offset, count_of_rows):
    heads_on_shard = peak.shape[0]
    hit = lax.broadcasted_iota(jnp.int32, (1, 1, dilation), 2) == start_offset.reshape(
        heads_on_shard, 1, 1
    )
    peak_full = jnp.where(hit, peak[:, :, None], NEG).reshape(heads_on_shard, count_of_rows)
    total_full = jnp.where(hit, total[:, :, None], 0.0).reshape(heads_on_shard, count_of_rows)
    summed_full = jnp.where(hit[:, :, :, None], summed[:, :, None, :], 0.0).reshape(
        heads_on_shard, count_of_rows, HEAD_DIM
    )
    return (peak_full, total_full, summed_full)


def local(queries, keys, values, offsets, out_weight):
    count_of_rows = queries.shape[0]
    heads_on_shard = queries.shape[1] // HEAD_DIM
    segment_width = heads_on_shard * HEAD_DIM
    shard_offsets = lax.dynamic_slice_in_dim(
        offsets, lax.axis_index("tp") * heads_on_shard, heads_on_shard, 0
    )
    nearby_offset = shard_offsets[:, 0] % SECOND_DILATION
    distant_offset = shard_offsets[:, 1] % THIRD_DILATION

    def heads_first(field):
        return field.reshape(field.shape[0], heads_on_shard, HEAD_DIM).transpose(1, 0, 2)

    local_parts = lax.map(attend, (heads_first(queries), heads_first(keys), heads_first(values)))
    nearby_query = select_rows(queries, SECOND_DILATION, nearby_offset, heads_on_shard)
    near_kv = jnp.stack(
        [
            select_rows(keys, SECOND_DILATION, nearby_offset, heads_on_shard).reshape(
                -1, segment_width
            ),
            select_rows(values, SECOND_DILATION, nearby_offset, heads_on_shard).reshape(
                -1, segment_width
            ),
        ]
    )
    for bit in range(SPAN_BITS):
        partner = partner_2(near_kv, "ctx", bit)
        near_kv = jnp.concatenate([near_kv, partner], axis=1)
    nearby_partials = lax.map(
        attend, (nearby_query.transpose(1, 0, 2), heads_first(near_kv[0]), heads_first(near_kv[1]))
    )
    nearby_partials = widen_pattern(
        nearby_partials[0],
        nearby_partials[1],
        nearby_partials[2],
        SECOND_DILATION,
        nearby_offset,
        count_of_rows,
    )
    distant_query = select_rows(queries, THIRD_DILATION, distant_offset, heads_on_shard).transpose(
        1, 0, 2
    )
    far_kv = jnp.stack(
        [
            select_rows(keys, THIRD_DILATION, distant_offset, heads_on_shard).reshape(
                -1, segment_width
            ),
            select_rows(values, THIRD_DILATION, distant_offset, heads_on_shard).reshape(
                -1, segment_width
            ),
        ]
    )
    far_rows = distant_query.shape[1]
    piece = lax.all_gather(far_kv, "ctx", axis=1, tiled=True)
    fold_peak = jnp.full((heads_on_shard, far_rows), NEG, jnp.float32)
    piece_k = heads_first(piece[0])
    piece_v = heads_first(piece[1])
    scores = jnp.einsum(
        "hld,hsd->hls", distant_query, piece_k, preferred_element_type=jnp.float32
    ) * HEAD_DIM ** (-0.5)
    new_peak = jnp.maximum(fold_peak, jnp.max(scores, axis=2))
    expo = jnp.exp(scores - new_peak[:, :, None])
    fold_total = jnp.sum(expo, axis=2)
    fold_summed = jnp.einsum(
        "hls,hsd->hld", expo.astype(jnp.bfloat16), piece_v, preferred_element_type=jnp.float32
    )
    distant_partials = (new_peak, fold_total, fold_summed)
    distant_partials = widen_pattern(
        distant_partials[0],
        distant_partials[1],
        distant_partials[2],
        THIRD_DILATION,
        distant_offset,
        count_of_rows,
    )
    parts = [local_parts, nearby_partials, distant_partials]
    top = jnp.maximum(jnp.maximum(parts[0][0], parts[1][0]), parts[2][0])
    numer = jnp.zeros((heads_on_shard, count_of_rows, HEAD_DIM), jnp.float32)
    denom = jnp.zeros((heads_on_shard, count_of_rows), jnp.float32)
    for peak, total, summed in parts:
        factor = jnp.exp(peak - top)
        numer = numer + factor[:, :, None] * summed
        denom = denom + factor * total
    attn = (
        (numer / denom[:, :, None])
        .astype(jnp.bfloat16)
        .transpose(1, 0, 2)
        .reshape(count_of_rows, segment_width)
    )
    mixed = lax.psum_scatter(
        jnp.dot(attn, out_weight, preferred_element_type=jnp.float32).astype(jnp.bfloat16),
        "tp",
        scatter_dimension=0,
        tiled=True,
    )
    return mixed


def solution(mesh):
    return jax.shard_map(
        local,
        mesh=mesh,
        in_specs=(P("ctx", "tp"), P("ctx", "tp"), P("ctx", "tp"), P(), P("tp", None)),
        out_specs=P(("ctx", "tp"), None),
        check_vma=False,
    )
```

profile of v0, /device:TPU:1, one launch (start us, length us, event | category | flops | bytes accessed | tf_op | source)
XLA Modules:
  0.0 332.6 jit_solution(5016633176902496921)
XLA Ops:
  7.5 4.0 %reshape.280 = bf16[64,16,8,64]{3,2,1,0:T(8,128)(2,1)} reshape(bf16[1024,512]{1,0:T(8,128)(2,1)} %param.9) | data formatting | bytes 2097152 | tf_op jit(solution)/shard_map/reshape | solution.py:19
  11.4 3.9 %reshape.281 = bf16[64,16,8,64]{3,2,1,0:T(8,128)(2,1)} reshape(bf16[1024,512]{1,0:T(8,128)(2,1)} %param.10) | data formatting | bytes 2097152 | tf_op jit(solution)/shard_map/reshape | solution.py:19
  15.3 2.1 reshape.282
  17.4 6.0 %select_reduce_fusion.2 = (bf16[64,8,64]{2,1,0:T(8,128)(2,1)}, bf16[64,8,64]{2,1,0:T(8,128)(2,1)S(1)}, bf16[64,8,64]{2,1,0:T(8,128)(2,1)S(1)}) fusion(bf16[64,16,8,64]{3,2,1,0:T(8,128)(2,1)} %reshape.280, pred[16,8]{1,0:T(8,128)(4,1)S(1)} %iota_compare_fusion, bf16[64,16,8,64]{3,2,1,0:T(8,128)(2,1)} %reshape.281, bf16[64,16,8,64]{3,2,1,0:T(8,128)(2,1)} %reshape.282), kind=kLoop, calls=%fused_computation.51 | loop fusion | flops 3047424 | bytes 3342464 | tf_op jit(solution)/shard_map/reduce_sum | solution.py:23
  23.7 1.0 pad_maximum_fusion.4
  24.7 2.1 reshape.277
  26.8 3.9 %reshape.278 = bf16[128,8,8,64]{3,2,1,0:T(8,128)(2,1)} reshape(bf16[1024,512]{1,0:T(8,128)(2,1)} %param.10) | data formatting | bytes 2097152 | tf_op jit(solution)/shard_map/reshape | solution.py:19
  30.7 3.9 %reshape.279 = bf16[128,8,8,64]{3,2,1,0:T(8,128)(2,1)} reshape(bf16[1024,512]{1,0:T(8,128)(2,1)} %param.11) | data formatting | bytes 2097152 | tf_op jit(solution)/shard_map/reshape | solution.py:19
  34.6 6.4 %select_reduce_fusion.4 = (bf16[128,8,64]{2,1,0:T(8,128)(2,1)S(1)}, bf16[128,8,64]{2,1,0:T(8,128)(2,1)}, bf16[128,8,64]{2,1,0:T(8,128)(2,1)}) fusion(bf16[128,8,8,64]{3,2,1,0:T(8,128)(2,1)} %reshape.278, pred[8,8]{1,0:T(8,128)(4,1)S(1)} %get-tuple-element.179, bf16[128,8,8,64]{3,2,1,0:T(8,128)(2,1)} %reshape.279, bf16[128,8,8,64]{3,2,1,0:T(8,128)(2,1)} %reshape.277), kind=kLoop, calls=%fused_computation.53 | loop fusion | flops 2949120 | bytes 3539008 | tf_op jit(solution)/shard_map/reduce_sum | solution.py:23
  41.2 1.1 copy.38
  42.4 3.8 %collective-permute-start = (bf16[2,128,512]{1,2,0:T(8,128)(2,1)S(1)}, bf16[2,128,512]{1,2,0:T(8,128)(2,1)S(1)}, u32[]{:S(2)}, u32[]{:S(2)}) collective-permute-start(bf16[2,128,512]{1,2,0:T(8,128)(2,1)S(1)} %pad_maximum_fusion.3), channel_id=1, source_target_pairs={{0,4},{4,0},{8,12},{12,8},{16,20},{20,16},{24,28},{28,24},{32,36},... | collective-permute-start | bytes 786440 | tf_op jit(solution)/shard_map/ppermute | solution.py:14
  46.2 5.0 %collective-permute-done = bf16[2,128,512]{1,2,0:T(8,128)(2,1)S(1)} collective-permute-done((bf16[2,128,512]{1,2,0:T(8,128)(2,1)S(1)}, bf16[2,128,512]{1,2,0:T(8,128)(2,1)S(1)}, u32[]{:S(2)}, u32[]{:S(2)}) %collective-permute-start) | collective-permute-done | bytes 262176 | tf_op jit(solution)/shard_map/ppermute | solution.py:14
  52.8 2.4 collective-permute-start.1
  55.2 1.3 copy.30
  56.5 1.5 copy.31
  58.0 2.3 copy.32
  60.4 7.5 %collective-permute-done.1 = bf16[2,256,512]{1,2,0:T(8,128)(2,1)} collective-permute-done((bf16[2,256,512]{1,2,0:T(8,128)(2,1)}, bf16[2,256,512]{1,2,0:T(8,128)(2,1)}, u32[]{:S(2)}, u32[]{:S(2)}) %collective-permute-start.1) | collective-permute-done | bytes 524320 | tf_op jit(solution)/shard_map/ppermute | solution.py:14
  67.8 2.2 pad_maximum_fusion.1
  70.0 3.2 collective-permute-start.2
  73.2 40.8 %while.30 = (s32[]{:T(128)}, f32[8,1024]{1,0:T(8,128)S(1)}, f32[8,1024]{1,0:T(8,128)S(1)}, f32[8,1024,64]{1,2,0:T(8,128)}, bf16[8,1024,64]{1,2,0:T(8,128)(2,1)},...) while((s32[]{:T(128)}, f32[8,1024]{1,0:T(8,128)S(1)}, f32[8,1024]{1,0:T(8,128)S(1)}, ...), condition=%wide.region_3.4_spmd.clone, body=%wide.region_0.3_spmd.sunk.clone | while | flops 276822016 | bytes 13273173 | solution.py:64
  73.2 1.7 multiply_reduce_fusion.4
  74.9 2.4 fusion.78
  78.3 1.7 multiply_reduce_fusion.4
  80.0 2.4 fusion.78
  83.4 1.7 multiply_reduce_fusion.4
  85.1 2.5 fusion.78
  88.5 1.7 multiply_reduce_fusion.4
  90.2 2.5 fusion.78
  93.6 1.7 multiply_reduce_fusion.4
  95.3 2.4 fusion.78
  98.7 1.7 multiply_reduce_fusion.4
  100.4 2.5 fusion.78
  103.9 1.7 multiply_reduce_fusion.4
  105.5 2.5 fusion.78
  109.0 1.7 multiply_reduce_fusion.4
  110.6 2.5 fusion.78
  114.1 1.7 copy.39
  116.5 3.8 %copy.46 = f32[8,1024,64]{2,1,0:T(8,128)} copy(f32[8,1024,64]{1,2,0:T(8,128)} %get-tuple-element.85) | data formatting | bytes 4194304 | tf_op jit(solution)/shard_map/while | solution.py:64
  120.3 5.2 %collective-permute-done.2 = bf16[2,512,512]{1,2,0:T(8,128)(2,1)} collective-permute-done((bf16[2,512,512]{1,2,0:T(8,128)(2,1)}, bf16[2,512,512]{1,2,0:T(8,128)(2,1)}, u32[]{:S(2)}, u32[]{:S(2)}) %collective-permute-start.2) | collective-permute-done | bytes 1048608 | tf_op jit(solution)/shard_map/ppermute | solution.py:14
  125.5 1.6 pad_maximum_fusion
  127.1 1.1 fusion.52
  128.3 19.4 %while.31 = (s32[]{:T(128)}, f32[8,128]{1,0:T(8,128)S(1)}, f32[8,128]{1,0:T(8,128)S(1)}, f32[8,128,64]{1,2,0:T(8,128)}, bf16[8,128,64]{2,1,0:T(8,128)(2,1)}, /*i...) while((s32[]{:T(128)}, f32[8,128]{1,0:T(8,128)S(1)}, f32[8,128]{1,0:T(8,128)S(1)}, ...), condition=%wide.region_10.11_spmd.clone, body=%wide.region_7.10_spmd.sunk.clone | while | flops 34340608 | bytes 1906773 | solution.py:79
  128.3 1.2 fusion.81
  130.7 1.2 fusion.81
  133.1 1.2 fusion.81
  135.5 1.2 fusion.81
  138.0 1.2 fusion.81
  140.4 1.2 fusion.81
  141.6 0.9 fusion.83
  142.8 1.2 fusion.81
  145.3 1.2 fusion.81
  148.6 1.2 copy.47
  149.8 45.6 %all-gather.2.cloned.1.call-done = bf16[2,4096,512]{2,0,1:T(2,128)(2,1)} async-done(((bf16[2,64,512]{2,0,1:T(2,128)(2,1)}), bf16[2,4096,512]{2,0,1:T(2,128)(2,1)}) %all-gather.2.cloned.1.call-update) | async-done | bytes 8388624 | tf_op jit(solution)/shard_map/all_gather | solution.py:104
  195.4 17.1 %fusion.51 = (bf16[1,4096,512]{2,0,1:T(2,128)(2,1)}, bf16[1,4096,512]{2,0,1:T(2,128)(2,1)}) fusion(bf16[2,4096,512]{2,0,1:T(2,128)(2,1)} %all-gather.2.cloned.1.call-done), kind=kLoop, calls=%fused_computation.82 | loop fusion | bytes 16777216 | tf_op jit(solution)/shard_map/slice | solution.py:107
  212.5 18.5 %copy.44 = bf16[1,4096,512]{1,2,0:T(8,128)(2,1)} copy(bf16[1,4096,512]{2,0,1:T(2,128)(2,1)} %get-tuple-element.174) | data formatting | bytes 8388608 | tf_op jit(solution)/shard_map/slice | solution.py:106
  231.0 3.5 %multiply_reduce_fusion.1 = (f32[8,64]{1,0:T(8,128)S(1)}, f32[8,64,4096]{2,1,0:T(8,128)S(1)}) fusion(bf16[8,4096,64]{1,2,0:T(8,128)(2,1)} %bitcast.134, bf16[8,64,64]{2,0,1:T(8,128)(2,1)S(1)} %bitcast.153), kind=kOutput, calls=%fused_computation.33 | convolution fusion | flops 272629248 | bytes 12650496 | tf_op jit(solution)/shard_map/hld,hsd->hls/dot_general | solution.py:108
  234.5 1.5 fusion.33
  236.0 1.7 copy-done.1
  238.3 18.4 %copy.48 = bf16[1,4096,512]{1,2,0:T(8,128)(2,1)} copy(bf16[1,4096,512]{2,0,1:T(2,128)(2,1)} %get-tuple-element.173) | data formatting | bytes 8388608 | tf_op jit(solution)/shard_map/slice | solution.py:107
  256.7 6.3 %fusion.35 = f32[8,64,64]{2,1,0:T(8,128)S(1)} fusion(bf16[8,4096,64]{1,2,0:T(8,128)(2,1)} %bitcast.135, f32[8,64,4096]{2,1,0:T(8,128)} %copy-done.1, f32[8,64]{1,0:T(8,128)S(1)} %broadcast_maximum_fusion), kind=kOutput, calls=%fused_computation.36 | convolution fusion | flops 274726912 | bytes 12716032 | tf_op jit(solution)/shard_map/hls,hsd->hld/dot_general | solution.py:114
  263.1 8.9 %fusion.44 = bf16[8,1024,64]{2,1,0:T(8,128)(2,1)} fusion(f32[8,1024,64]{2,1,0:T(8,128)S(1)} %copy-done.2, f32[8,1024]{1,0:T(8,128)S(1)} %get-tuple-element.165, f32[8,64,64]{2,1,0:T(8,128)S(1)} %fusion.35, f32[8,1024]{1,0:T(8,128)S(1)} %get-tuple-element.168, f32[8,128,64]{2,1,0:T(8,128)S(1)} %copy.47, f32[8,1024]{1,0:T(8,128)S(1)} %get-tuple-element.167, ...), kind=kLoop, calls=%fused_computation.46 | loop fusion | flops 4718592 | bytes 3686400 | tf_op jit(solution)/shard_map/convert_element_type | solution.py:136
  272.0 1.9 copy.49
  273.9 4.3 %convolution_convert_fusion = bf16[1024,2048]{1,0:T(8,128)(2,1)} fusion(bf16[1024,512]{0,1:T(8,128)(2,1)S(1)} %bitcast.151, bf16[512,2048]{1,0:T(8,128)(2,1)S(1)} %copy-done), kind=kOutput, calls=%fused_computation.47 | convolution fusion | flops 2149580800 | bytes 7340032 | tf_op jit(solution)/shard_map/dot_general | solution.py:141
  278.3 47.5 %reduce-scatter.2.cloned.1.call-done = bf16[256,2048]{1,0:T(8,128)(2,1)} async-done(((bf16[1024,2048]{1,0:T(8,128)(2,1)}), bf16[256,2048]{1,0:T(8,128)(2,1)}) %reduce-scatter.2.cloned.1.call-update) | async-done | bytes 1048592 | tf_op jit(solution)/shard_map/reduce_scatter | solution.py:140
  (104 shorter events, 21.6 us)
Async XLA Ops:
  6.5 267.4 %copy-start = (bf16[512,2048]{1,0:T(8,128)(2,1)S(1)}, bf16[512,2048]{1,0:T(8,128)(2,1)}, u32[]{:S(2)}) copy-start(bf16[512,2048]{1,0:T(8,128)(2,1)} %param.13) | copy-start | bytes 6291460
  6.5 8.8 %copy-start.4 = (bf16[1024,512]{1,0:T(8,128)(2,1)S(1)}, bf16[1024,512]{1,0:T(8,128)(2,1)}, u32[]{:S(2)}) copy-start(bf16[1024,512]{1,0:T(8,128)(2,1)} %param.11) | copy-start | bytes 3145732
  6.5 188.8 %all-gather.2.cloned.1.call-start = ((), (), s32[]{:S(2)}) async-start(), calls=%async_computation.1 | async-start | bytes 8519680 | tf_op jit(solution)/shard_map/all_gather | solution.py:104
  17.4 7.3 %copy-start.3 = (bf16[1024,512]{1,0:T(8,128)(2,1)S(1)}, bf16[1024,512]{1,0:T(8,128)(2,1)}, u32[]{:S(2)}) copy-start(bf16[1024,512]{1,0:T(8,128)(2,1)} %param.9) | copy-start | bytes 3145732
  24.6 301.1 %reduce-scatter.2.cloned.1.call-start = ((), (), s32[]{:S(2)}) async-start(), calls=%async_computation.2 | async-start | bytes 5242880 | tf_op jit(solution)/shard_map/reduce_scatter | solution.py:140
  42.4 8.8 %collective-permute-start = (bf16[2,128,512]{1,2,0:T(8,128)(2,1)S(1)}, bf16[2,128,512]{1,2,0:T(8,128)(2,1)S(1)}, u32[]{:S(2)}, u32[]{:S(2)}) collective-permute-start(bf16[2,128,512]{1,2,0:T(8,128)(2,1)S(1)} %pad_maximum_fusion.3), channel_id=1, source_target_pairs={{0,4},{4,0},{8,12},{12,8},{16,20},{20,16},{24,28},{28,24},{32,36},... | collective-permute-start | bytes 786440 | tf_op jit(solution)/shard_map/ppermute | solution.py:14
  51.2 0.7 copy-start.5
  52.8 15.0 %collective-permute-start.1 = (bf16[2,256,512]{1,2,0:T(8,128)(2,1)}, bf16[2,256,512]{1,2,0:T(8,128)(2,1)}, u32[]{:S(2)}, u32[]{:S(2)}) collective-permute-start(bf16[2,256,512]{1,2,0:T(8,128)(2,1)} %pad_maximum_fusion.2), channel_id=1, source_target_pairs={{0,8},{4,12},{8,0},{12,4},{16,24},{20,28},{24,16},{28,20},{32,40},... | collective-permute-start | bytes 1572872 | tf_op jit(solution)/shard_map/ppermute | solution.py:14
  70.0 55.5 %collective-permute-start.2 = (bf16[2,512,512]{1,2,0:T(8,128)(2,1)}, bf16[2,512,512]{1,2,0:T(8,128)(2,1)}, u32[]{:S(2)}, u32[]{:S(2)}) collective-permute-start(bf16[2,512,512]{1,2,0:T(8,128)(2,1)} %pad_maximum_fusion.1), channel_id=1, source_target_pairs={{0,16},{4,20},{8,24},{12,28},{16,0},{20,4},{24,8},{28,12},{32,48},... | collective-permute-start | bytes 3145736 | tf_op jit(solution)/shard_map/ppermute | solution.py:14
  114.1 11.4 %copy-start.6 = (bf16[2,128,512]{1,2,0:T(8,128)(2,1)S(1)}, bf16[2,128,512]{1,2,0:T(8,128)(2,1)}, u32[]{:S(2)}) copy-start(bf16[2,128,512]{1,2,0:T(8,128)(2,1)} %copy-done.5) | copy-start | bytes 786436
  212.5 18.5 %copy-start.7 = (bf16[64,8,64]{2,1,0:T(8,128)(2,1)S(1)}, bf16[64,8,64]{2,1,0:T(8,128)(2,1)}, u32[]{:S(2)}) copy-start(bf16[64,8,64]{2,1,0:T(8,128)(2,1)} %get-tuple-element.131) | copy-start | bytes 196612
  234.5 3.2 copy-start.1
  256.7 6.3 %copy-start.2 = (f32[8,1024,64]{2,1,0:T(8,128)S(1)}, f32[8,1024,64]{2,1,0:T(8,128)}, u32[]{:S(2)}) copy-start(f32[8,1024,64]{2,1,0:T(8,128)} %copy.46) | copy-start | bytes 6291460
Sparse Core Ops, SparseCore 0:
  24.8 170.5 all-gather.1
  278.4 47.2 reduce-scatter.1
where the time goes:
time: 334 us; the launch traced here: 333 us
  waiting for transfers between devices  111 us (33%)
  local copies, waits for them, and re-layouts  97.9 us (29%)
  matrix products  64 us (19%)
  other arithmetic  36.3 us (11%)
  between operations  13.6 us (4%)
  starting transfers between devices  9.53 us (3%)
    reduce_scatter x1, waiting for transfers between devices, local(): lax.psum_scatter(jnp.dot(attn, out_weight, preferred_element_type=jnp.flo...  47.5 us
    all_gather x1, waiting for transfers between devices, local(): piece = lax.all_gather(far_kv, 'ctx', axis=1, tiled=True)  45.6 us
    slice x2, local copies, waits for them, and re-layouts, local(): piece_v = heads_first(piece[1])  35.5 us
    dot_general x16, matrix products, attend(): jnp.dot(expo.astype(jnp.bfloat16), value_per_head, preferred_element_type...  26.9 us
    dot_general x16, matrix products, attend(): jnp.dot(query_per_head, key_per_head.T, preferred_element_type=jnp.float32)  23.1 us
    reshape x6, local copies, waits for them, and re-layouts, select_rows(): field.reshape(count_of_rows // dilation, dilation, heads_on_shard, HEAD_DIM)  19.8 us
    slice x1, local copies, waits for them, and re-layouts, local(): piece_k = heads_first(piece[0])  18.5 us
    ppermute x3, waiting for transfers between devices, partner_2(): lax.ppermute(shard, axis, [(i, i ^ 1 << stride) for i in range(lax.axis_s...  17.6 us
  transfers between devices with their start and end apart: 5, of which 5 were waited for; matrix products, arithmetic and copies ran while one was open for 29% of the time, Pallas kernels for 0%

commit v1 on v0

--- a/solution.py
+++ b/solution.py
@@ -101,7 +101,10 @@
         ]
     )
     far_rows = distant_query.shape[1]
-    piece = lax.all_gather(far_kv, "ctx", axis=1, tiled=True)
+    n_dev = lax.axis_size("ctx")
+    pieces = jnp.stack([far_kv for _ in range(n_dev)])
+    pieces = lax.all_to_all(pieces, "ctx", split_axis=0, concat_axis=0)
+    piece = jnp.concatenate(pieces, axis=1)
     fold_peak = jnp.full((heads_on_shard, far_rows), NEG, jnp.float32)
     piece_k = heads_first(piece[0])
     piece_v = heads_first(piece[1])

time: 334 us -> 442 us (1.32)
  waiting for transfers between devices: 111 us -> 214 us
  starting transfers between devices: 9.53 us -> 22.1 us
  matrix products: 64 us -> 59.2 us
    ppermute x3, waiting for transfers between devices: 17.6 us -> 163 us  [partner_2(): lax.ppermute(shard, axis, [(i, i ^ 1 << stride) for i in range(lax.axis_s...]
    another operation x0 -> x5, local copies, waits for them, and re-layouts: none -> 46.2 us  [the longest x4 41.9 us: heads_first(): field.reshape(field.shape[0], heads_on_shard, HEAD_DIM).transpose(1, 0, 2)]
    all_gather x1 -> x0, waiting for transfers between devices: 45.6 us -> none  [local(): piece = lax.all_gather(far_kv, 'ctx', axis=1, tiled=True)]
    slice x2 -> x1, local copies, waits for them, and re-layouts: 35.5 us -> 5.96 us  [local(): piece_v = heads_first(piece[1])]
    slice x1 -> x0, local copies, waits for them, and re-layouts: 18.5 us -> none  [local(): piece_k = heads_first(piece[0])]
    all_to_all x0 -> x1, starting transfers between devices: none -> 15.5 us  [local(): pieces = lax.all_to_all(pieces, 'ctx', split_axis=0, concat_axis=0)]
    dot_general x1, matrix products: 6.28 us -> 1.58 us  [local(): jnp.einsum('hls,hsd->hld', expo.astype(jnp.bfloat16), piece_v, preferred_...]
  transfers between devices with their start and end apart: 5 -> 5, of which waited for: 5 -> 3; matrix products, arithmetic and copies ran while one was open for 29% -> 22% of each run, Pallas kernels for 0% -> 0%
where the time goes in v1:
time: 442 us; the launch traced here: 440 us
  waiting for transfers between devices  214 us (48%)
  local copies, waits for them, and re-layouts  94.6 us (21%)
  matrix products  59.2 us (13%)
  other arithmetic  36.4 us (8%)
  starting transfers between devices  22.1 us (5%)
  between operations  13.6 us (3%)
    ppermute x3, waiting for transfers between devices, partner_2(): lax.ppermute(shard, axis, [(i, i ^ 1 << stride) for i in range(lax.axis_s...  163 us
    reduce_scatter x1, waiting for transfers between devices, local(): lax.psum_scatter(jnp.dot(attn, out_weight, preferred_element_type=jnp.flo...  51.2 us
    another operation x4, local copies, waits for them, and re-layouts, heads_first(): field.reshape(field.shape[0], heads_on_shard, HEAD_DIM).transpose(1, 0, 2)  41.9 us
    dot_general x16, matrix products, attend(): jnp.dot(expo.astype(jnp.bfloat16), value_per_head, preferred_element_type...  26.8 us
    dot_general x16, matrix products, attend(): jnp.dot(query_per_head, key_per_head.T, preferred_element_type=jnp.float32)  23.1 us
    reshape x6, local copies, waits for them, and re-layouts, select_rows(): field.reshape(count_of_rows // dilation, dilation, heads_on_shard, HEAD_DIM)  19.9 us
    all_to_all x1, starting transfers between devices, local(): pieces = lax.all_to_all(pieces, 'ctx', split_axis=0, concat_axis=0)  15.5 us
    reduce_sum x2, other arithmetic, select_rows(): return jnp.sum(jnp.where(picked, shaped, jnp.zeros_like(shaped)), axis=1)  12.3 us
  transfers between devices with their start and end apart: 5, of which 3 were waited for; matrix products, arithmetic and copies ran while one was open for 22% of the time, Pallas kernels for 0%

profile of v1, /device:TPU:1, one launch (start us, length us, event | category | flops | bytes accessed | tf_op | source)
XLA Modules:
  0.0 440.3 jit_solution(14819962510180356459)
XLA Ops:
  7.5 4.0 reshape.290
  11.4 3.9 reshape.291
  15.3 2.1 reshape.292
  17.4 5.9 %select_reduce_fusion.2 = (bf16[64,8,64]{2,1,0:T(8,128)(2,1)}, bf16[64,8,64]{2,1,0:T(8,128)(2,1)S(1)}, bf16[64,8,64]{2,1,0:T(8,128)(2,1)S(1)}) fusion(bf16[64,16,8,64]{3,2,1,0:T(8,128)(2,1)} %reshape.290, pred[16,8]{1,0:T(8,128)(4,1)S(1)} %iota_compare_fusion, bf16[64,16,8,64]{3,2,1,0:T(8,128)(2,1)} %reshape.291, bf16[64,16,8,64]{3,2,1,0:T(8,128)(2,1)} %reshape.292), kind=kLoop, calls=%fused_computation.54 | loop fusion | flops 3047424 | bytes 3342464 | tf_op jit(solution)/shard_map/reduce_sum | solution.py:23
  23.7 4.3 stack.8
  27.9 15.5 %all-to-all-start = ((bf16[64,2,64,512]{3,2,1,0:T(8,128)(2,1)}), bf16[64,2,64,512]{3,2,1,0:T(8,128)(2,1)}, u32[]{:S(2)}, u32[]{:S(2)}) async-start(bf16[64,2,64,512]{3,2,1,0:T(8,128)(2,1)} %stack.8), calls=%async_computation | async-start | bytes 16777216 | tf_op jit(solution)/shard_map/all_to_all | solution.py:106
  43.7 2.1 reshape.287
  45.8 3.9 reshape.288
  49.7 3.9 reshape.289
  53.7 6.4 %select_reduce_fusion.4 = (bf16[128,8,64]{2,1,0:T(8,128)(2,1)S(1)}, bf16[128,8,64]{2,1,0:T(8,128)(2,1)}, bf16[128,8,64]{2,1,0:T(8,128)(2,1)}) fusion(bf16[128,8,8,64]{3,2,1,0:T(8,128)(2,1)} %reshape.288, pred[8,8]{1,0:T(8,128)(4,1)S(1)} %get-tuple-element.179, bf16[128,8,8,64]{3,2,1,0:T(8,128)(2,1)} %reshape.289, bf16[128,8,8,64]{3,2,1,0:T(8,128)(2,1)} %reshape.287), kind=kLoop, calls=%fused_computation.56 | loop fusion | flops 2949120 | bytes 3539008 | tf_op jit(solution)/shard_map/reduce_sum | solution.py:23
  60.3 1.1 copy.42
  61.5 2.5 collective-permute-start
  64.0 9.0 %collective-permute-done = bf16[2,128,512]{1,2,0:T(8,128)(2,1)S(1)} collective-permute-done((bf16[2,128,512]{1,2,0:T(8,128)(2,1)S(1)}, bf16[2,128,512]{1,2,0:T(8,128)(2,1)S(1)}, u32[]{:S(2)}, u32[]{:S(2)}) %collective-permute-start) | collective-permute-done | bytes 262176 | tf_op jit(solution)/shard_map/ppermute | solution.py:14
  74.6 2.1 collective-permute-start.1
  76.7 1.3 copy.34
  78.0 1.5 copy.35
  79.5 2.3 copy.36
  81.8 153.6 %collective-permute-done.1 = bf16[2,256,512]{1,2,0:T(8,128)(2,1)} collective-permute-done((bf16[2,256,512]{1,2,0:T(8,128)(2,1)}, bf16[2,256,512]{1,2,0:T(8,128)(2,1)}, u32[]{:S(2)}, u32[]{:S(2)}) %collective-permute-start.1) | collective-permute-done | bytes 524320 | tf_op jit(solution)/shard_map/ppermute | solution.py:14
  235.4 2.2 pad_maximum_fusion.1
  237.6 1.8 collective-permute-start.2
  239.3 40.5 %while.30 = (s32[]{:T(128)}, f32[8,1024]{1,0:T(8,128)S(1)}, f32[8,1024]{1,0:T(8,128)S(1)}, f32[8,1024,64]{1,2,0:T(8,128)}, bf16[8,1024,64]{1,2,0:T(8,128)(2,1)},...) while((s32[]{:T(128)}, f32[8,1024]{1,0:T(8,128)S(1)}, f32[8,1024]{1,0:T(8,128)S(1)}, ...), condition=%wide.region_3.4_spmd.clone, body=%wide.region_0.3_spmd.sunk.clone | while | flops 276822016 | bytes 13273181 | solution.py:64
  239.3 1.7 multiply_reduce_fusion.4
  241.7 2.4 fusion.78
  244.4 1.7 multiply_reduce_fusion.4
  246.8 2.4 fusion.78
  249.4 1.7 multiply_reduce_fusion.4
  251.8 2.4 fusion.78
  254.5 1.7 multiply_reduce_fusion.4
  256.9 2.5 fusion.78
  259.6 1.7 multiply_reduce_fusion.4
  262.0 2.4 fusion.78
  264.6 1.7 multiply_reduce_fusion.4
  267.0 2.5 fusion.78
  269.7 1.7 multiply_reduce_fusion.4
  272.1 2.4 fusion.78
  274.7 1.7 multiply_reduce_fusion.4
  277.2 2.4 fusion.78
  280.5 1.7 copy.43
  282.2 3.8 copy.48
  286.0 1.6 pad_maximum_fusion
  287.6 1.1 fusion.54
  288.7 19.4 %while.31 = (s32[]{:T(128)}, f32[8,128]{1,0:T(8,128)S(1)}, f32[8,128]{1,0:T(8,128)S(1)}, f32[8,128,64]{1,2,0:T(8,128)}, bf16[8,128,64]{2,1,0:T(8,128)(2,1)}, /*i...) while((s32[]{:T(128)}, f32[8,128]{1,0:T(8,128)S(1)}, f32[8,128]{1,0:T(8,128)S(1)}, ...), condition=%wide.region_10.11_spmd.clone, body=%wide.region_7.10_spmd.sunk.clone | while | flops 34340608 | bytes 1906781 | solution.py:79
  288.7 1.2 fusion.81
  291.2 1.2 fusion.81
  293.6 1.2 fusion.81
  296.0 1.2 fusion.81
  298.4 1.2 fusion.81
  299.9 0.9 fusion.83
  300.8 1.2 fusion.81
  303.3 1.2 fusion.81
  305.7 1.2 fusion.81
  308.1 1.1 copy.49
  310.2 6.0 %fusion.53 = (bf16[1,64,64,512]{3,2,0,1:T(8,128)(2,1)}, bf16[1,64,64,512]{3,2,0,1:T(8,128)(2,1)}) fusion(bf16[2,64,64,512]{3,2,0,1:T(8,128)(2,1)} %bitcast.28), kind=kLoop, calls=%fused_computation.84 | loop fusion | bytes 16777216 | tf_op jit(solution)/shard_map/slice | solution.py:110
  316.2 11.2 %reshape_squeeze.15 = bf16[4096,8,64]{2,1,0:T(8,128)(2,1)} reshape(bf16[1,64,64,512]{3,2,0,1:T(8,128)(2,1)} %get-tuple-element.173) | data formatting | bytes 8388608 | tf_op jit(solution)/shard_map/reshape;squeeze | solution.py:62
  327.3 9.8 %copy.50 = bf16[4096,8,64]{0,2,1:T(8,128)(2,1)} copy(bf16[4096,8,64]{2,1,0:T(8,128)(2,1)} %reshape_squeeze.15) | data formatting | bytes 8388608 | tf_op jit(solution)/shard_map/reshape;squeeze | solution.py:62
  337.1 11.2 %reshape_squeeze.14 = bf16[4096,8,64]{2,1,0:T(8,128)(2,1)} reshape(bf16[1,64,64,512]{3,2,0,1:T(8,128)(2,1)} %get-tuple-element.174) | data formatting | bytes 8388608 | tf_op jit(solution)/shard_map/reshape;squeeze | solution.py:62
  348.3 9.8 %copy.46 = bf16[4096,8,64]{0,2,1:T(8,128)(2,1)} copy(bf16[4096,8,64]{2,1,0:T(8,128)(2,1)} %reshape_squeeze.14) | data formatting | bytes 8388608 | tf_op jit(solution)/shard_map/reshape;squeeze | solution.py:62
  358.1 3.5 multiply_reduce_fusion.1
  361.6 1.5 fusion.33
  363.8 1.6 fusion.35
  366.0 9.9 %fusion.47 = bf16[8,1024,64]{2,1,0:T(8,128)(2,1)} fusion(f32[8,1024,64]{2,1,0:T(8,128)} %copy.48, f32[8,1024]{1,0:T(8,128)S(1)} %get-tuple-element.165, f32[8,64,64]{2,1,0:T(8,128)S(1)} %fusion.35, f32[8,1024]{1,0:T(8,128)S(1)} %get-tuple-element.168, f32[8,128,64]{2,1,0:T(8,128)S(1)} %copy.49, f32[8,1024]{1,0:T(8,128)S(1)} %get-tuple-element.167, ...), kind=kLoop, calls=%fused_computation.49 | loop fusion | flops 4718592 | bytes 3686400 | tf_op jit(solution)/shard_map/convert_element_type | solution.py:139
  375.9 1.9 copy.51
  377.9 4.3 convolution_convert_fusion
  382.2 51.2 %reduce-scatter.2.cloned.1.call-done = bf16[256,2048]{1,0:T(8,128)(2,1)} async-done(((bf16[1024,2048]{1,0:T(8,128)(2,1)}), bf16[256,2048]{1,0:T(8,128)(2,1)}) %reduce-scatter.2.cloned.1.call-update) | async-done | bytes 1048592 | tf_op jit(solution)/shard_map/reduce_scatter | solution.py:143
  (104 shorter events, 22.2 us)
Async XLA Ops:
  6.5 371.3 %copy-start = (bf16[512,2048]{1,0:T(8,128)(2,1)S(1)}, bf16[512,2048]{1,0:T(8,128)(2,1)}, u32[]{:S(2)}) copy-start(bf16[512,2048]{1,0:T(8,128)(2,1)} %param.13) | copy-start | bytes 6291460
  6.5 8.8 %copy-start.3 = (bf16[1024,512]{1,0:T(8,128)(2,1)S(1)}, bf16[1024,512]{1,0:T(8,128)(2,1)}, u32[]{:S(2)}) copy-start(bf16[1024,512]{1,0:T(8,128)(2,1)} %param.11) | copy-start | bytes 3145732
  27.9 15.8 %copy-start.2 = (bf16[1024,512]{1,0:T(8,128)(2,1)S(1)}, bf16[1024,512]{1,0:T(8,128)(2,1)}, u32[]{:S(2)}) copy-start(bf16[1024,512]{1,0:T(8,128)(2,1)} %param.9) | copy-start | bytes 3145732
  27.9 282.3 %all-to-all-start = ((bf16[64,2,64,512]{3,2,1,0:T(8,128)(2,1)}), bf16[64,2,64,512]{3,2,1,0:T(8,128)(2,1)}, u32[]{:S(2)}, u32[]{:S(2)}) async-start(bf16[64,2,64,512]{3,2,1,0:T(8,128)(2,1)} %stack.8), calls=%async_computation | async-start | bytes 16777216 | tf_op jit(solution)/shard_map/all_to_all | solution.py:106
  43.4 390.0 %reduce-scatter.2.cloned.1.call-start = ((), (), s32[]{:S(2)}) async-start(), calls=%async_computation.2 | async-start | bytes 5242880 | tf_op jit(solution)/shard_map/reduce_scatter | solution.py:143
  61.5 11.5 %collective-permute-start = (bf16[2,128,512]{1,2,0:T(8,128)(2,1)S(1)}, bf16[2,128,512]{1,2,0:T(8,128)(2,1)S(1)}, u32[]{:S(2)}, u32[]{:S(2)}) collective-permute-start(bf16[2,128,512]{1,2,0:T(8,128)(2,1)S(1)} %pad_maximum_fusion.3), channel_id=1, source_target_pairs={{0,4},{4,0},{8,12},{12,8},{16,20},{20,16},{24,28},{28,24},{32,36},... | collective-permute-start | bytes 786440 | tf_op jit(solution)/shard_map/ppermute | solution.py:14
  73.0 0.7 copy-start.4
  74.6 160.8 %collective-permute-start.1 = (bf16[2,256,512]{1,2,0:T(8,128)(2,1)}, bf16[2,256,512]{1,2,0:T(8,128)(2,1)}, u32[]{:S(2)}, u32[]{:S(2)}) collective-permute-start(bf16[2,256,512]{1,2,0:T(8,128)(2,1)} %pad_maximum_fusion.2), channel_id=1, source_target_pairs={{0,8},{4,12},{8,0},{12,4},{16,24},{20,28},{24,16},{28,20},{32,40},... | collective-permute-start | bytes 1572872 | tf_op jit(solution)/shard_map/ppermute | solution.py:14
  237.6 48.4 %collective-permute-start.2 = (bf16[2,512,512]{1,2,0:T(8,128)(2,1)}, bf16[2,512,512]{1,2,0:T(8,128)(2,1)}, u32[]{:S(2)}, u32[]{:S(2)}) collective-permute-start(bf16[2,512,512]{1,2,0:T(8,128)(2,1)} %pad_maximum_fusion.1), channel_id=1, source_target_pairs={{0,16},{4,20},{8,24},{12,28},{16,0},{20,4},{24,8},{28,12},{32,48},... | collective-permute-start | bytes 3145736 | tf_op jit(solution)/shard_map/ppermute | solution.py:14
  279.8 6.2 %copy-start.5 = (bf16[2,128,512]{1,2,0:T(8,128)(2,1)S(1)}, bf16[2,128,512]{1,2,0:T(8,128)(2,1)}, u32[]{:S(2)}) copy-start(bf16[2,128,512]{1,2,0:T(8,128)(2,1)} %copy-done.4) | copy-start | bytes 786436
  348.3 9.8 %copy-start.6 = (bf16[64,8,64]{2,1,0:T(8,128)(2,1)S(1)}, bf16[64,8,64]{2,1,0:T(8,128)(2,1)}, u32[]{:S(2)}) copy-start(bf16[64,8,64]{2,1,0:T(8,128)(2,1)} %get-tuple-element.131) | copy-start | bytes 196612
  361.6 2.2 copy-start.1
Sparse Core Ops, SparseCore 0:
  382.3 51.0 reduce-scatter.1
